TPU v7x, 32 devices: a whole 2x2x4 slice. The times are simulated.
32 devices in a mesh: dp: 4 (over y, x), expert: 8 (over z, core).
Axes of the slice: x: 2, y: 2, z: 4, core: 2. Of those that a mesh axis runs over, the one named last changes fastest.
Arguments:
- tokens: bfloat16 [4096, 2048], P(('dp', 'expert')), may hold values from -6 to 6
- cotangent: bfloat16 [4096, 2048], P(('dp', 'expert')), may hold values from -1.5 to 1.5
- expert_ids: int32 [4096, 8], P(('dp', 'expert')), may hold values from 0 to 127, as said below
- gate_values: float32 [4096, 8], P(('dp', 'expert')), may hold values from 0.1 to 0.5
- w_gate: bfloat16 [2048, 8, 768], P(None, 'expert'), may hold values from -0.125 to 0.125
- w_up: bfloat16 [2048, 8, 768], P(None, 'expert'), may hold values from -0.125 to 0.125
- w_down: bfloat16 [2048, 8, 768], P(None, 'expert'), may hold values from -0.21875 to 0.21875
Outputs:
- output: bfloat16 [4096, 2048], P(('dp', 'expert'))
- grad_input: bfloat16 [4096, 2048], P(('dp', 'expert'))
- grad_gate: float32 [2048, 8, 768], P('dp', 'expert')
- grad_up: float32 [2048, 8, 768], P('dp', 'expert')
- grad_down: float32 [2048, 8, 768], P('dp', 'expert')
Inputs may be any that keep to these rules, and one draw needn't show every extreme that they name: `expert_ids`: each row names 8 different experts in any order. In the rows of one device no expert under 8 is named more than 32 times; in each group of 1024 rows (one index of dp) one expert under 8 is named exactly 32 times by the rows of every device of the group.
All inputs are finite; a program needn't handle non-finite values.
Results may differ from a plain program's by a relative error of at most 0.013.
Values may be sent and summed in bfloat16 or wider, within the bound.
A program may use at most 128 MiB of HBM per device.

v0:
```python
import functools

import jax
import jax.numpy as jnp
from jax import lax
from jax.experimental import pallas as pl
from jax.experimental.pallas import tpu as pltpu
from jax.sharding import PartitionSpec as P

MESH = pl.DeviceIdType.MESH
F32 = jnp.float32
BF16 = jnp.bfloat16


def dot(a, b, dims=((1,), (0,))):
    return lax.dot_general(a, b, (dims, ((), ())), preferred_element_type=F32)


def tile_of(size):
    return 256 if size % 256 == 0 else 128


def kernel(
    owners, groups, cap,
    tokens, cotangent, ids, gates, wg_hbm, wu_hbm, wd_hbm,
    output, grad_input, x_cols, z_cols, hid_all, dg_all, du_all,
    wg, wu, wd, x_send, z_send, x_rows, z_rows, out_send, dx_send, out_back, dx_back,
    hid, dg, du, gate_pre, up_pre, sel, gate_hi, gate_lo,
    w_sem, self_sem, own_sem,
    x_ss, x_rs, z_ss, z_rs, o_ss, o_rs, d_ss, d_rs,
    c_ss, c_rs,
):
    me = lax.axis_index("expert")
    my_dp = lax.axis_index("dp")
    toks, width = tokens.shape
    slots = owners * cap
    hidden_units = hid.shape[1]
    cols = width // groups

    loads = [
        pltpu.make_async_copy(src, dst, w_sem.at[i])
        for i, (src, dst) in enumerate(((wg_hbm, wg), (wu_hbm, wu), (wd_hbm, wd)))
    ]
    for load in loads:
        load.start()

    barrier = pltpu.get_barrier_semaphore()
    for i in range(1, owners):
        pl.semaphore_signal(
            barrier, inc=1, device_id={"expert": lax.rem(me + i, owners)}, device_id_type=MESH
        )
    for i in range(1, groups):
        pl.semaphore_signal(
            barrier, inc=1, device_id={"dp": lax.rem(my_dp + i, groups)}, device_id_type=MESH
        )

    lanes = 128
    expert = lax.broadcasted_iota(jnp.int32, (toks, lanes), 1)
    present = jnp.zeros((toks, lanes), F32)
    gate = jnp.zeros((toks, lanes), F32)
    for k in range(ids.shape[1]):
        hit = ids[:, k : k + 1] == expert
        present = jnp.where(hit, 1.0, present)
        gate = jnp.where(hit, gates[:, k : k + 1], gate)
    row = lax.broadcasted_iota(jnp.int32, (toks, toks), 0)
    col = lax.broadcasted_iota(jnp.int32, (toks, toks), 1)
    before = jnp.where(col < row, 1.0, 0.0).astype(BF16)
    rank = dot(before, present.astype(BF16))
    rank = jnp.where(present > 0.0, rank, -1.0)
    spread = jnp.where(
        lax.broadcasted_iota(jnp.int32, (lanes, slots), 1) // cap
        == lax.broadcasted_iota(jnp.int32, (lanes, slots), 0),
        1.0,
        0.0,
    ).astype(BF16)
    rank_at = dot(rank.astype(BF16), spread)
    place = lax.rem(lax.broadcasted_iota(jnp.int32, (toks, slots), 1), cap).astype(F32)
    chosen = jnp.where(rank_at == place, 1.0, 0.0)
    hi = gate.astype(BF16)
    lo = (gate - hi.astype(F32)).astype(BF16)
    hi_at = dot(hi, spread) * chosen
    lo_at = dot(lo, spread) * chosen
    sel[...] = chosen.astype(BF16)
    gate_hi[...] = hi_at.astype(BF16)
    gate_lo[...] = lo_at.astype(BF16)
    sel_t = chosen.T.astype(BF16)
    hi_t = hi_at.T.astype(BF16)
    lo_t = lo_at.T.astype(BF16)
    dt = tile_of(width)

    @pl.loop(0, width // dt)
    def _(i):
        at = pl.ds(pl.multiple_of(i * dt, dt), dt)
        x_send[:, at] = dot(sel_t, tokens[:, at]).astype(BF16)

    def block(r):
        return pl.ds(pl.multiple_of(r * cap, cap), cap)

    def exchange(src, dst, ss, rs, own):
        copies = [pltpu.make_async_copy(src.at[block(me), :], dst.at[block(me), :], own)]
        for i in range(1, owners):
            peer = lax.rem(me + i, owners)
            copies.append(
                pltpu.make_async_remote_copy(
                    src_ref=src.at[block(peer), :],
                    dst_ref=dst.at[block(me), :],
                    send_sem=ss.at[i - 1],
                    recv_sem=rs.at[i - 1],
                    device_id={"expert": peer},
                    device_id_type=MESH,
                )
            )
        for c in copies:
            c.start()
        return copies

    def share(n, src_of, dst):
        copies = [pltpu.make_async_copy(src_of(my_dp), dst.at[my_dp], own_sem.at[n])]
        for i in range(1, groups):
            peer = lax.rem(my_dp + i, groups)
            copies.append(
                pltpu.make_async_remote_copy(
                    src_ref=src_of(peer),
                    dst_ref=dst.at[my_dp],
                    send_sem=c_ss.at[n, i - 1],
                    recv_sem=c_rs.at[n, i - 1],
                    device_id={"dp": peer},
                    device_id_type=MESH,
                )
            )
        for c in copies:
            c.start()
        return copies

    def finish(copies):
        for c in copies:
            c.wait()

    def columns(ref):
        return lambda g: ref.at[:, pl.ds(pl.multiple_of(g * cols, cols), cols)]

    pl.semaphore_wait(barrier, owners + groups - 2)
    x_copies = exchange(x_send, x_rows, x_ss, x_rs, self_sem.at[0])

    @pl.loop(0, width // dt)
    def _(i):
        at = pl.ds(pl.multiple_of(i * dt, dt), dt)
        c = cotangent[:, at]
        z_send[:, at] = (dot(hi_t, c) + dot(lo_t, c)).astype(BF16)

    z_copies = exchange(z_send, z_rows, z_ss, z_rs, self_sem.at[1])

    finish(loads)
    finish(x_copies)
    shared = share(0, columns(x_rows), x_cols)

    ft = tile_of(hidden_units)

    @pl.loop(0, hidden_units // ft)
    def _(i):
        at = pl.ds(pl.multiple_of(i * ft, ft), ft)
        g = dot(x_rows[...], wg[:, at])
        u = dot(x_rows[...], wu[:, at])
        gate_pre[:, at] = g
        up_pre[:, at] = u
        hid[:, at] = (g * lax.logistic(g) * u).astype(BF16)

    shared += share(1, lambda g: hid, hid_all)

    @pl.loop(0, width // dt)
    def _(i):
        at = pl.ds(pl.multiple_of(i * dt, dt), dt)
        out_send[:, at] = dot(hid[...], wd[at, :], ((1,), (1,))).astype(BF16)

    finish(z_copies)
    shared += share(2, columns(z_rows), z_cols)
    o_copies = exchange(out_send, out_back, o_ss, o_rs, self_sem.at[2])

    @pl.loop(0, hidden_units // ft)
    def _(i):
        at = pl.ds(pl.multiple_of(i * ft, ft), ft)
        dh = dot(z_rows[...], wd[:, at])
        g = gate_pre[:, at]
        s = lax.logistic(g)
        dg[:, at] = (dh * up_pre[:, at] * s * (1.0 + g * (1.0 - s))).astype(BF16)
        du[:, at] = (dh * g * s).astype(BF16)

    shared += share(3, lambda g: dg, dg_all)
    shared += share(4, lambda g: du, du_all)

    @pl.loop(0, width // dt)
    def _(i):
        at = pl.ds(pl.multiple_of(i * dt, dt), dt)
        dx_send[:, at] = (
            dot(dg[...], wg[at, :], ((1,), (1,))) + dot(du[...], wu[at, :], ((1,), (1,)))
        ).astype(BF16)

    d_copies = exchange(dx_send, dx_back, d_ss, d_rs, self_sem.at[3])

    finish(o_copies)

    @pl.loop(0, width // dt)
    def _(i):
        at = pl.ds(pl.multiple_of(i * dt, dt), dt)
        r = out_back[:, at]
        output[:, at] = (dot(gate_hi[...], r) + dot(gate_lo[...], r)).astype(BF16)

    finish(d_copies)

    @pl.loop(0, width // dt)
    def _(i):
        at = pl.ds(pl.multiple_of(i * dt, dt), dt)
        grad_input[:, at] = dot(sel[...], dx_back[:, at]).astype(BF16)

    finish(shared)


def per_device(tokens, cotangent, expert_ids, gate_values, w_gate, w_up, w_down):
    owners = lax.axis_size("expert")
    groups = lax.axis_size("dp")
    toks, width = tokens.shape
    cap = toks // 4
    local, units = w_gate.shape[1:]
    assert local == 1
    slots = owners * cap
    cols = width // groups
    vmem = pl.BlockSpec(memory_space=pltpu.VMEM)
    hbm = pl.BlockSpec(memory_space=pl.ANY)
    rows = pltpu.VMEM((slots, width), BF16)
    acts = pltpu.VMEM((slots, units), BF16)
    weight = pltpu.VMEM((width, units), BF16)
    wide = pltpu.VMEM((slots, units), F32)
    table = pltpu.VMEM((toks, slots), BF16)
    dma = pltpu.SemaphoreType.DMA
    out, dx, x_cols, z_cols, hid, dg, du = pl.pallas_call(
        functools.partial(kernel, owners, groups, cap),
        out_shape=[jax.ShapeDtypeStruct((toks, width), BF16)] * 2
        + [jax.ShapeDtypeStruct((groups, slots, cols), BF16)] * 2
        + [jax.ShapeDtypeStruct((groups, slots, units), BF16)] * 3,
        in_specs=[vmem] * 4 + [hbm] * 3,
        out_specs=[vmem] * 2 + [hbm] * 5,
        scratch_shapes=[weight] * 3
        + [rows] * 8
        + [acts] * 3
        + [wide] * 2
        + [table] * 3
        + [dma((3,)), dma((4,)), dma((5,))]
        + [dma((owners - 1,))] * 8
        + [dma((5, groups - 1))] * 2,
        compiler_params=pltpu.CompilerParams(
            collective_id=0, has_side_effects=True, vmem_limit_bytes=50 * 2**20
        ),
        name="moe",
    )(
        tokens, cotangent, expert_ids, gate_values,
        w_gate[:, 0], w_up[:, 0], w_down[:, 0],
    )

    def grad(a, b):
        return jnp.einsum("gsd,gsf->df", a, b, preferred_element_type=F32)[:, None, :]

    return out, dx, grad(x_cols, dg), grad(x_cols, du), grad(z_cols, hid)


def solution(mesh):
    rows = P(("dp", "expert"), None)
    held = P(None, "expert", None)
    grads = P("dp", "expert", None)
    return jax.shard_map(
        per_device,
        mesh=mesh,
        in_specs=(rows, rows, rows, rows, held, held, held),
        out_specs=(rows, rows, grads, grads, grads),
        check_vma=False,
    )
```

profile of v0, /device:TPU:13, one launch (start us, length us, event | category | flops | bytes accessed | tf_op | source)
XLA Modules:
  0.0 132.5 jit_solution(5169634554589900655)
XLA Ops:
  0.6 0.8 copy.12.ids
  1.4 0.8 copy.13.gates
  2.2 0.0 copy-start
  2.2 1.0 copy-done
  3.2 0.0 copy-start.1
  3.2 1.0 copy-done.1
  4.3 113.7 %moe.1 = (bf16[128,2048]{1,0:T(8,128)(2,1)S(1)}, bf16[128,2048]{1,0:T(8,128)(2,1)S(1)}, bf16[4,256,512]{2,1,0:T(8,128)(2,1)S(1)}, bf16[4,256,512]{2,1,0:T(8,128)...) custom-call(bf16[128,2048]{1,0:T(8,128)(2,1)S(1)} %copy-done, ...), custom_call_target="tpu_custom_call" | custom-call | tf_op jit(solution)/shard_map/moe/pallas_call | solution.py:235
  117.9 0.0 copy-start.3
  118.0 2.6 %convolution_bitcast_fusion.2 = f32[512,1,768]{2,0,1:T(8,128)S(1)} fusion(bf16[4,256,512]{2,1,0:T(8,128)(2,1)S(1)} %get-tuple-element.14, bf16[4,256,768]{2,1,0:T(8,128)(2,1)} %get-tuple-element.15), kind=kOutput, calls=%fused_computation.2 | convolution fusion | flops 805306368 | bytes 4194304 | tf_op jit(solution)/shard_map/gsd,gsf->df/dot_general | solution.py:260
  120.5 0.0 copy-done.3
  120.5 1.0 convolution_bitcast_fusion.1
  121.6 2.8 %copy.18 = f32[512,1,768]{2,1,0:T(1,128)} copy(f32[512,1,768]{2,0,1:T(8,128)S(1)} %convolution_bitcast_fusion.1) | data formatting | bytes 3145728
  124.3 0.0 copy-start.2
  124.3 0.0 copy-start.4
  124.3 2.8 %copy.17 = f32[512,1,768]{2,1,0:T(1,128)} copy(f32[512,1,768]{2,0,1:T(8,128)S(1)} %convolution_bitcast_fusion.2) | data formatting | bytes 3145728
  127.1 0.0 copy-done.2
  127.1 0.0 copy-done.4
  127.1 1.0 convolution_bitcast_fusion
  128.1 2.8 %copy.19 = f32[512,1,768]{2,1,0:T(1,128)} copy(f32[512,1,768]{2,0,1:T(8,128)S(1)} %convolution_bitcast_fusion) | data formatting | bytes 3145728
  130.9 0.8 copy.25
  131.7 0.8 copy.26
Async XLA Ops:
  2.2 1.0 copy-start
  3.2 1.0 copy-start.1
  117.9 2.6 %copy-start.3 = (bf16[4,256,768]{2,1,0:T(8,128)(2,1)S(1)}, bf16[4,256,768]{2,1,0:T(8,128)(2,1)}, u32[]{:S(2)}) copy-start(bf16[4,256,768]{2,1,0:T(8,128)(2,1)} %get-tuple-element.16) | copy-start | bytes 4718596
  124.3 2.8 %copy-start.2 = (bf16[4,256,768]{2,1,0:T(8,128)(2,1)S(1)}, bf16[4,256,768]{2,1,0:T(8,128)(2,1)}, u32[]{:S(2)}) copy-start(bf16[4,256,768]{2,1,0:T(8,128)(2,1)} %get-tuple-element.18) | copy-start | bytes 4718596
  124.3 2.8 %copy-start.4 = (bf16[4,256,512]{2,1,0:T(8,128)(2,1)S(1)}, bf16[4,256,512]{2,1,0:T(8,128)(2,1)}, u32[]{:S(2)}) copy-start(bf16[4,256,512]{2,1,0:T(8,128)(2,1)} %get-tuple-element.17) | copy-start | bytes 3145732
where the time goes:
time: 133 us; the launch traced here: 132 us
  Pallas kernels  114 us (86%)
  local copies, waits for them, and re-layouts  13.5 us (10%)
  matrix products  4.6 us (3%)
    pallas_call x1, Pallas kernels, per_device(): pl.pallas_call(functools.partial(kernel, owners, groups, cap), out_shape=...  114 us
    unnamed x17, local copies, waits for them, and re-layouts  13.5 us
    dot_general x3, matrix products, grad(): jnp.einsum('gsd,gsf->df', a, b, preferred_element_type=F32)[:, None, :]  4.6 us

commit v1 on v0

--- a/solution.py
+++ b/solution.py
@@ -22,9 +22,9 @@
 
 def kernel(
     owners, groups, cap,
-    tokens, cotangent, ids, gates, wg_hbm, wu_hbm, wd_hbm,
+    tok_hbm, cot_hbm, ids, gates, wg_hbm, wu_hbm, wd_hbm,
     output, grad_input, x_cols, z_cols, hid_all, dg_all, du_all,
-    wg, wu, wd, x_send, z_send, x_rows, z_rows, out_send, dx_send, out_back, dx_back,
+    tokens, cotangent, wg, wu, wd, x_send, z_send, x_rows, z_rows, out_send, dx_send, out_back, dx_back,
     hid, dg, du, gate_pre, up_pre, sel, gate_hi, gate_lo,
     w_sem, self_sem, own_sem,
     x_ss, x_rs, z_ss, z_rs, o_ss, o_rs, d_ss, d_rs,
@@ -39,7 +39,15 @@
 
     loads = [
         pltpu.make_async_copy(src, dst, w_sem.at[i])
-        for i, (src, dst) in enumerate(((wg_hbm, wg), (wu_hbm, wu), (wd_hbm, wd)))
+        for i, (src, dst) in enumerate(
+            (
+                (tok_hbm, tokens),
+                (cot_hbm, cotangent),
+                (wg_hbm, wg),
+                (wu_hbm, wu),
+                (wd_hbm, wd),
+            )
+        )
     ]
     for load in loads:
         load.start()
@@ -55,38 +63,37 @@
         )
 
     lanes = 128
-    expert = lax.broadcasted_iota(jnp.int32, (toks, lanes), 1)
-    present = jnp.zeros((toks, lanes), F32)
-    gate = jnp.zeros((toks, lanes), F32)
-    for k in range(ids.shape[1]):
-        hit = ids[:, k : k + 1] == expert
+    expert = lax.broadcasted_iota(jnp.int32, (lanes, toks), 0)
+    present = jnp.zeros((lanes, toks), F32)
+    gate = jnp.zeros((lanes, toks), F32)
+    for k in range(ids.shape[0]):
+        hit = ids[k : k + 1, :] == expert
         present = jnp.where(hit, 1.0, present)
-        gate = jnp.where(hit, gates[:, k : k + 1], gate)
+        gate = jnp.where(hit, gates[k : k + 1, :], gate)
     row = lax.broadcasted_iota(jnp.int32, (toks, toks), 0)
     col = lax.broadcasted_iota(jnp.int32, (toks, toks), 1)
-    before = jnp.where(col < row, 1.0, 0.0).astype(BF16)
-    rank = dot(before, present.astype(BF16))
+    before = jnp.where(row < col, 1.0, 0.0).astype(BF16)
+    rank = dot(present.astype(BF16), before)
     rank = jnp.where(present > 0.0, rank, -1.0)
     spread = jnp.where(
-        lax.broadcasted_iota(jnp.int32, (lanes, slots), 1) // cap
-        == lax.broadcasted_iota(jnp.int32, (lanes, slots), 0),
+        lax.broadcasted_iota(jnp.int32, (slots, lanes), 0) // cap
+        == lax.broadcasted_iota(jnp.int32, (slots, lanes), 1),
         1.0,
         0.0,
     ).astype(BF16)
-    rank_at = dot(rank.astype(BF16), spread)
-    place = lax.rem(lax.broadcasted_iota(jnp.int32, (toks, slots), 1), cap).astype(F32)
+    rank_at = dot(spread, rank.astype(BF16))
+    place = lax.rem(lax.broadcasted_iota(jnp.int32, (slots, toks), 0), cap).astype(F32)
     chosen = jnp.where(rank_at == place, 1.0, 0.0)
     hi = gate.astype(BF16)
     lo = (gate - hi.astype(F32)).astype(BF16)
-    hi_at = dot(hi, spread) * chosen
-    lo_at = dot(lo, spread) * chosen
-    sel[...] = chosen.astype(BF16)
-    gate_hi[...] = hi_at.astype(BF16)
-    gate_lo[...] = lo_at.astype(BF16)
-    sel_t = chosen.T.astype(BF16)
-    hi_t = hi_at.T.astype(BF16)
-    lo_t = lo_at.T.astype(BF16)
+    hi_at = dot(spread, hi) * chosen
+    lo_at = dot(spread, lo) * chosen
+    sel_t = chosen.astype(BF16)
+    hi_t = hi_at.astype(BF16)
+    lo_t = lo_at.astype(BF16)
     dt = tile_of(width)
+
+    loads[0].wait()
 
     @pl.loop(0, width // dt)
     def _(i):
@@ -98,8 +105,11 @@
 
     def exchange(src, dst, ss, rs, own):
         copies = [pltpu.make_async_copy(src.at[block(me), :], dst.at[block(me), :], own)]
-        for i in range(1, owners):
-            peer = lax.rem(me + i, owners)
+        half = owners // 2
+        side, spot = me // half, lax.rem(me, half)
+        peers = [(1 - side) * half + lax.rem(spot + i, half) for i in range(half)]
+        peers += [side * half + lax.rem(spot + i, half) for i in range(1, half)]
+        for i, peer in enumerate(peers, 1):
             copies.append(
                 pltpu.make_async_remote_copy(
                     src_ref=src.at[block(peer), :],
@@ -142,6 +152,8 @@
     pl.semaphore_wait(barrier, owners + groups - 2)
     x_copies = exchange(x_send, x_rows, x_ss, x_rs, self_sem.at[0])
 
+    loads[1].wait()
+
     @pl.loop(0, width // dt)
     def _(i):
         at = pl.ds(pl.multiple_of(i * dt, dt), dt)
@@ -150,7 +162,10 @@
 
     z_copies = exchange(z_send, z_rows, z_ss, z_rs, self_sem.at[1])
 
-    finish(loads)
+    sel[...] = chosen.T.astype(BF16)
+    gate_hi[...] = hi_at.T.astype(BF16)
+    gate_lo[...] = lo_at.T.astype(BF16)
+    finish(loads[2:])
     finish(x_copies)
     shared = share(0, columns(x_rows), x_cols)
 
@@ -213,6 +228,54 @@
         grad_input[:, at] = dot(sel[...], dx_back[:, at]).astype(BF16)
 
     finish(shared)
+
+
+def weight_grads(
+    out_in, dx_in, x_in, z_in, dg_in, du_in, hid_in,
+    out, dx, grad_gate, grad_up, grad_down,
+    x, z, dg, du, hid, panel_gate, panel_up, panel_down, in_sem, out_sem,
+):
+    loads = [
+        pltpu.make_async_copy(a, b, in_sem.at[i])
+        for i, (a, b) in enumerate(
+            ((x_in, x), (dg_in, dg), (du_in, du), (z_in, z), (hid_in, hid))
+        )
+    ]
+    stores = [
+        pltpu.make_async_copy(a, b, out_sem.at[i])
+        for i, (a, b) in enumerate(
+            (
+                (out_in, out),
+                (dx_in, dx),
+                (panel_gate, grad_gate),
+                (panel_up, grad_up),
+                (panel_down, grad_down),
+            )
+        )
+    ]
+    for c in loads + stores[:2]:
+        c.start()
+    cols, units = x.shape[1], dg.shape[1]
+    lines = units // 128
+    ft = tile_of(units)
+    for n, (a, b, panel, needs) in enumerate(
+        (
+            (x, dg, panel_gate, loads[:2]),
+            (x, du, panel_up, loads[2:3]),
+            (z, hid, panel_down, loads[3:]),
+        )
+    ):
+        for c in needs:
+            c.wait()
+        for f in range(0, units, ft):
+            total = dot(a[...], b[:, f : f + ft], ((0,), (0,)))
+            for j in range(ft // 128):
+                panel[pl.ds(f // 128 + j, cols, stride=lines), :] = total[
+                    :, j * 128 : (j + 1) * 128
+                ]
+        stores[2 + n].start()
+    for c in stores:
+        c.wait()
 
 
 def per_device(tokens, cotangent, expert_ids, gate_values, w_gate, w_up, w_down):
@@ -237,29 +300,41 @@
         out_shape=[jax.ShapeDtypeStruct((toks, width), BF16)] * 2
         + [jax.ShapeDtypeStruct((groups, slots, cols), BF16)] * 2
         + [jax.ShapeDtypeStruct((groups, slots, units), BF16)] * 3,
-        in_specs=[vmem] * 4 + [hbm] * 3,
+        in_specs=[hbm] * 2 + [vmem] * 2 + [hbm] * 3,
         out_specs=[vmem] * 2 + [hbm] * 5,
-        scratch_shapes=[weight] * 3
+        scratch_shapes=[pltpu.VMEM((toks, width), BF16)] * 2
+        + [weight] * 3
         + [rows] * 8
         + [acts] * 3
         + [wide] * 2
         + [table] * 3
-        + [dma((3,)), dma((4,)), dma((5,))]
+        + [dma((5,)), dma((4,)), dma((5,))]
         + [dma((owners - 1,))] * 8
         + [dma((5, groups - 1))] * 2,
         compiler_params=pltpu.CompilerParams(
-            collective_id=0, has_side_effects=True, vmem_limit_bytes=50 * 2**20
+            collective_id=0, has_side_effects=True, vmem_limit_bytes=58 * 2**20
         ),
         name="moe",
     )(
-        tokens, cotangent, expert_ids, gate_values,
+        tokens, cotangent, expert_ids.T, gate_values.T,
         w_gate[:, 0], w_up[:, 0], w_down[:, 0],
     )
 
-    def grad(a, b):
-        return jnp.einsum("gsd,gsf->df", a, b, preferred_element_type=F32)[:, None, :]
-
-    return out, dx, grad(x_cols, dg), grad(x_cols, du), grad(z_cols, hid)
+    flat = [a.reshape(groups * slots, -1) for a in (x_cols, z_cols, dg, du, hid)]
+    lines = units // 128
+    panel = jax.ShapeDtypeStruct((cols * lines, 128), F32)
+    out, dx, *panels = pl.pallas_call(
+        weight_grads,
+        out_shape=[jax.ShapeDtypeStruct((toks, width), BF16)] * 2 + [panel] * 3,
+        in_specs=[hbm] * 7,
+        out_specs=[hbm] * 5,
+        scratch_shapes=[pltpu.VMEM(a.shape, BF16) for a in flat]
+        + [pltpu.VMEM(panel.shape, F32)] * 3
+        + [dma((5,)), dma((5,))],
+        compiler_params=pltpu.CompilerParams(vmem_limit_bytes=58 * 2**20),
+        name="weight_grads",
+    )(out, dx, *flat)
+    return out, dx, *(p.reshape(cols, 1, units) for p in panels)
 
 
 def solution(mesh):

time: 133 us -> 151 us (1.14)
  Pallas kernels: 114 us -> 149 us
  local copies, waits for them, and re-layouts: 13.5 us -> 0 us
  matrix products: 4.6 us -> 0 us
    pallas_call x0 -> x1, Pallas kernels: none -> 33 us  [per_device(): pl.pallas_call(weight_grads, out_shape=[jax.ShapeDtypeStruct((toks, width...]
    unnamed x17 -> x0, local copies, waits for them, and re-layouts: 13.5 us -> none
    dot_general x3 -> x0, matrix products: 4.6 us -> none  [grad(): jnp.einsum('gsd,gsf->df', a, b, preferred_element_type=F32)[:, None, :]]
    pallas_call x1, Pallas kernels: 114 us -> 116 us  [per_device(): pl.pallas_call(functools.partial(kernel, owners, groups, cap), out_shape=...]
where the time goes in v1:
time: 151 us; the launch traced here: 150 us
  Pallas kernels  149 us (99%)
    pallas_call x1, Pallas kernels, per_device(): pl.pallas_call(functools.partial(kernel, owners, groups, cap), out_shape=...  116 us
    pallas_call x1, Pallas kernels, per_device(): pl.pallas_call(weight_grads, out_shape=[jax.ShapeDtypeStruct((toks, width...  33 us

profile of v1, /device:TPU:13, one launch (start us, length us, event | category | flops | bytes accessed | tf_op | source)
XLA Modules:
  0.0 150.1 jit_solution(185387690236044452)
XLA Ops:
  0.6 116.4 %moe.1 = (bf16[128,2048]{1,0:T(8,128)(2,1)}, bf16[128,2048]{1,0:T(8,128)(2,1)}, bf16[4,256,512]{2,1,0:T(8,128)(2,1)}, bf16[4,256,512]{2,1,0:T(8,128)(2,1)}, bf16...) custom-call(bf16[128,2048]{1,0:T(8,128)(2,1)} %tok_hbm.1, ...), custom_call_target="tpu_custom_call" | custom-call | tf_op jit(solution)/shard_map/moe/pallas_call | solution.py:298
  117.1 33.0 %weight_grads.1 = (bf16[128,2048]{1,0:T(8,128)(2,1)}, bf16[128,2048]{1,0:T(8,128)(2,1)}, f32[3072,128]{1,0:T(8,128)}, f32[3072,128]{1,0:T(8,128)}, f32[3072,128]{1,0:T(8,128)}) custom-call(bf16[128,2048]{1,0:T(8,128)(2,1)} %get-tuple-element.17.out_in, bf16[128,2048]{1,0:T(8,128)(2,1)} %get-tuple-element.18.dx_in, bf16[1024,512]{1,0:T(8,128)(2,1)} %bitcast.19, ...), custom_call_target="tpu_custom_call" | custom-call | tf_op jit(solution)/shard_map/weight_grads/pallas_call | solution.py:326

commit v2 on v1

--- a/solution.py
+++ b/solution.py
@@ -103,43 +103,47 @@
     def block(r):
         return pl.ds(pl.multiple_of(r * cap, cap), cap)
 
+    half = owners // 2
+    side, spot = me // half, lax.rem(me, half)
+    near_peers = [side * half + lax.rem(spot + i, half) for i in range(1, half)]
+    far_peers = [(1 - side) * half + lax.rem(spot + i, half) for i in range(half)]
+
     def exchange(src, dst, ss, rs, own):
         copies = [pltpu.make_async_copy(src.at[block(me), :], dst.at[block(me), :], own)]
-        half = owners // 2
-        side, spot = me // half, lax.rem(me, half)
-        peers = [(1 - side) * half + lax.rem(spot + i, half) for i in range(half)]
-        peers += [side * half + lax.rem(spot + i, half) for i in range(1, half)]
-        for i, peer in enumerate(peers, 1):
+        for i, peer in enumerate(near_peers + far_peers):
             copies.append(
                 pltpu.make_async_remote_copy(
                     src_ref=src.at[block(peer), :],
                     dst_ref=dst.at[block(me), :],
-                    send_sem=ss.at[i - 1],
-                    recv_sem=rs.at[i - 1],
+                    send_sem=ss.at[i],
+                    recv_sem=rs.at[i],
                     device_id={"expert": peer},
                     device_id_type=MESH,
                 )
             )
+        return copies[:half], copies[half:]
+
+    def start(copies):
         for c in copies:
             c.start()
-        return copies
-
-    def share(n, src_of, dst):
-        copies = [pltpu.make_async_copy(src_of(my_dp), dst.at[my_dp], own_sem.at[n])]
+
+    def share(n, src_of, dst, rows):
+        copies = [
+            pltpu.make_async_copy(src_of(my_dp, rows), dst.at[my_dp, rows, :], own_sem.at[n])
+        ]
         for i in range(1, groups):
             peer = lax.rem(my_dp + i, groups)
             copies.append(
                 pltpu.make_async_remote_copy(
-                    src_ref=src_of(peer),
-                    dst_ref=dst.at[my_dp],
+                    src_ref=src_of(peer, rows),
+                    dst_ref=dst.at[my_dp, rows, :],
                     send_sem=c_ss.at[n, i - 1],
                     recv_sem=c_rs.at[n, i - 1],
                     device_id={"dp": peer},
                     device_id_type=MESH,
                 )
             )
-        for c in copies:
-            c.start()
+        start(copies)
         return copies
 
     def finish(copies):
@@ -147,10 +151,17 @@
             c.wait()
 
     def columns(ref):
-        return lambda g: ref.at[:, pl.ds(pl.multiple_of(g * cols, cols), cols)]
+        return lambda g, rows: ref.at[rows, pl.ds(pl.multiple_of(g * cols, cols), cols)]
+
+    def whole(ref):
+        return lambda g, rows: ref.at[rows, :]
 
     pl.semaphore_wait(barrier, owners + groups - 2)
     x_copies = exchange(x_send, x_rows, x_ss, x_rs, self_sem.at[0])
+    z_copies = exchange(z_send, z_rows, z_ss, z_rs, self_sem.at[1])
+    o_copies = exchange(out_send, out_back, o_ss, o_rs, self_sem.at[2])
+    d_copies = exchange(dx_send, dx_back, d_ss, d_rs, self_sem.at[3])
+    start(x_copies[0] + x_copies[1])
 
     loads[1].wait()
 
@@ -160,59 +171,71 @@
         c = cotangent[:, at]
         z_send[:, at] = (dot(hi_t, c) + dot(lo_t, c)).astype(BF16)
 
-    z_copies = exchange(z_send, z_rows, z_ss, z_rs, self_sem.at[1])
-
+    start(z_copies[0] + z_copies[1])
     sel[...] = chosen.T.astype(BF16)
     gate_hi[...] = hi_at.T.astype(BF16)
     gate_lo[...] = lo_at.T.astype(BF16)
     finish(loads[2:])
-    finish(x_copies)
-    shared = share(0, columns(x_rows), x_cols)
-
     ft = tile_of(hidden_units)
-
-    @pl.loop(0, hidden_units // ft)
-    def _(i):
-        at = pl.ds(pl.multiple_of(i * ft, ft), ft)
-        g = dot(x_rows[...], wg[:, at])
-        u = dot(x_rows[...], wu[:, at])
-        gate_pre[:, at] = g
-        up_pre[:, at] = u
-        hid[:, at] = (g * lax.logistic(g) * u).astype(BF16)
-
-    shared += share(1, lambda g: hid, hid_all)
-
-    @pl.loop(0, width // dt)
-    def _(i):
-        at = pl.ds(pl.multiple_of(i * dt, dt), dt)
-        out_send[:, at] = dot(hid[...], wd[at, :], ((1,), (1,))).astype(BF16)
-
-    finish(z_copies)
-    shared += share(2, columns(z_rows), z_cols)
-    o_copies = exchange(out_send, out_back, o_ss, o_rs, self_sem.at[2])
-
-    @pl.loop(0, hidden_units // ft)
-    def _(i):
-        at = pl.ds(pl.multiple_of(i * ft, ft), ft)
-        dh = dot(z_rows[...], wd[:, at])
-        g = gate_pre[:, at]
-        s = lax.logistic(g)
-        dg[:, at] = (dh * up_pre[:, at] * s * (1.0 + g * (1.0 - s))).astype(BF16)
-        du[:, at] = (dh * g * s).astype(BF16)
-
-    shared += share(3, lambda g: dg, dg_all)
-    shared += share(4, lambda g: du, du_all)
-
-    @pl.loop(0, width // dt)
-    def _(i):
-        at = pl.ds(pl.multiple_of(i * dt, dt), dt)
-        dx_send[:, at] = (
-            dot(dg[...], wg[at, :], ((1,), (1,))) + dot(du[...], wu[at, :], ((1,), (1,)))
-        ).astype(BF16)
-
-    d_copies = exchange(dx_send, dx_back, d_ss, d_rs, self_sem.at[3])
-
-    finish(o_copies)
+    part = slots // 2
+    shared = []
+
+    def forward(n, rows):
+        finish(x_copies[n])
+        shared.extend(share(5 * n, columns(x_rows), x_cols, rows))
+
+        @pl.loop(0, hidden_units // ft)
+        def _(i):
+            at = pl.ds(pl.multiple_of(i * ft, ft), ft)
+            g = dot(x_rows[rows, :], wg[:, at])
+            u = dot(x_rows[rows, :], wu[:, at])
+            gate_pre[rows, at] = g
+            up_pre[rows, at] = u
+            hid[rows, at] = (g * lax.logistic(g) * u).astype(BF16)
+
+        shared.extend(share(5 * n + 1, whole(hid), hid_all, rows))
+
+        @pl.loop(0, width // dt)
+        def _(i):
+            at = pl.ds(pl.multiple_of(i * dt, dt), dt)
+            out_send[rows, at] = dot(hid[rows, :], wd[at, :], ((1,), (1,))).astype(BF16)
+
+        start(o_copies[n])
+
+    def backward(n, rows):
+        finish(z_copies[n])
+        shared.extend(share(5 * n + 2, columns(z_rows), z_cols, rows))
+
+        @pl.loop(0, hidden_units // ft)
+        def _(i):
+            at = pl.ds(pl.multiple_of(i * ft, ft), ft)
+            dh = dot(z_rows[rows, :], wd[:, at])
+            g = gate_pre[rows, at]
+            s = lax.logistic(g)
+            dg[rows, at] = (dh * up_pre[rows, at] * s * (1.0 + g * (1.0 - s))).astype(BF16)
+            du[rows, at] = (dh * g * s).astype(BF16)
+
+        shared.extend(share(5 * n + 3, whole(dg), dg_all, rows))
+        shared.extend(share(5 * n + 4, whole(du), du_all, rows))
+
+        @pl.loop(0, width // dt)
+        def _(i):
+            at = pl.ds(pl.multiple_of(i * dt, dt), dt)
+            dx_send[rows, at] = (
+                dot(dg[rows, :], wg[at, :], ((1,), (1,)))
+                + dot(du[rows, :], wu[at, :], ((1,), (1,)))
+            ).astype(BF16)
+
+        start(d_copies[n])
+
+    near = pl.ds(pl.multiple_of(side * part, part), part)
+    far = pl.ds(pl.multiple_of((1 - side) * part, part), part)
+    forward(0, near)
+    backward(0, near)
+    forward(1, far)
+    backward(1, far)
+
+    finish(o_copies[0] + o_copies[1])
 
     @pl.loop(0, width // dt)
     def _(i):
@@ -220,7 +243,7 @@
         r = out_back[:, at]
         output[:, at] = (dot(gate_hi[...], r) + dot(gate_lo[...], r)).astype(BF16)
 
-    finish(d_copies)
+    finish(d_copies[0] + d_copies[1])
 
     @pl.loop(0, width // dt)
     def _(i):
@@ -233,27 +256,35 @@
 def weight_grads(
     out_in, dx_in, x_in, z_in, dg_in, du_in, hid_in,
     out, dx, grad_gate, grad_up, grad_down,
-    x, z, dg, du, hid, panel_gate, panel_up, panel_down, in_sem, out_sem,
+    out_at, dx_at, x, z, dg, du, hid, panel_gate, panel_up, panel_down, in_sem, out_sem,
 ):
     loads = [
         pltpu.make_async_copy(a, b, in_sem.at[i])
         for i, (a, b) in enumerate(
-            ((x_in, x), (dg_in, dg), (du_in, du), (z_in, z), (hid_in, hid))
+            (
+                (x_in, x),
+                (dg_in, dg),
+                (du_in, du),
+                (z_in, z),
+                (hid_in, hid),
+                (out_in, out_at),
+                (dx_in, dx_at),
+            )
         )
     ]
     stores = [
         pltpu.make_async_copy(a, b, out_sem.at[i])
         for i, (a, b) in enumerate(
             (
-                (out_in, out),
-                (dx_in, dx),
+                (out_at, out),
+                (dx_at, dx),
                 (panel_gate, grad_gate),
                 (panel_up, grad_up),
                 (panel_down, grad_down),
             )
         )
     ]
-    for c in loads + stores[:2]:
+    for c in loads:
         c.start()
     cols, units = x.shape[1], dg.shape[1]
     lines = units // 128
@@ -262,7 +293,7 @@
         (
             (x, dg, panel_gate, loads[:2]),
             (x, du, panel_up, loads[2:3]),
-            (z, hid, panel_down, loads[3:]),
+            (z, hid, panel_down, loads[3:5]),
         )
     ):
         for c in needs:
@@ -274,6 +305,9 @@
                     :, j * 128 : (j + 1) * 128
                 ]
         stores[2 + n].start()
+    for load, c in zip(loads[5:], stores):
+        load.wait()
+        c.start()
     for c in stores:
         c.wait()
 
@@ -308,9 +342,9 @@
         + [acts] * 3
         + [wide] * 2
         + [table] * 3
-        + [dma((5,)), dma((4,)), dma((5,))]
+        + [dma((5,)), dma((4,)), dma((10,))]
         + [dma((owners - 1,))] * 8
-        + [dma((5, groups - 1))] * 2,
+        + [dma((10, groups - 1))] * 2,
         compiler_params=pltpu.CompilerParams(
             collective_id=0, has_side_effects=True, vmem_limit_bytes=58 * 2**20
         ),
@@ -328,9 +362,9 @@
         out_shape=[jax.ShapeDtypeStruct((toks, width), BF16)] * 2 + [panel] * 3,
         in_specs=[hbm] * 7,
         out_specs=[hbm] * 5,
-        scratch_shapes=[pltpu.VMEM(a.shape, BF16) for a in flat]
+        scratch_shapes=[pltpu.VMEM(a.shape, BF16) for a in (out, dx, *flat)]
         + [pltpu.VMEM(panel.shape, F32)] * 3
-        + [dma((5,)), dma((5,))],
+        + [dma((7,)), dma((5,))],
         compiler_params=pltpu.CompilerParams(vmem_limit_bytes=58 * 2**20),
         name="weight_grads",
     )(out, dx, *flat)

time: 151 us -> 109 us (0.72)
  Pallas kernels: 149 us -> 106 us
    pallas_call x1, Pallas kernels: 33 us -> 6.88 us  [per_device(): pl.pallas_call(weight_grads, out_shape=[jax.ShapeDtypeStruct((toks, width...]
    pallas_call x1, Pallas kernels: 116 us -> 99.3 us  [per_device(): pl.pallas_call(functools.partial(kernel, owners, groups, cap), out_shape=...]
where the time goes in v2:
time: 109 us; the launch traced here: 107 us
  Pallas kernels  106 us (97%)
    pallas_call x1, Pallas kernels, per_device(): pl.pallas_call(functools.partial(kernel, owners, groups, cap), out_shape=...  99.3 us
    pallas_call x1, Pallas kernels, per_device(): pl.pallas_call(weight_grads, out_shape=[jax.ShapeDtypeStruct((toks, width...  6.88 us

profile of v2, /device:TPU:13, one launch (start us, length us, event | category | flops | bytes accessed | tf_op | source)
XLA Modules:
  0.0 106.8 jit_solution(3388396503803862904)
XLA Ops:
  0.6 99.3 %moe.1 = (bf16[128,2048]{1,0:T(8,128)(2,1)}, bf16[128,2048]{1,0:T(8,128)(2,1)}, bf16[4,256,512]{2,1,0:T(8,128)(2,1)}, bf16[4,256,512]{2,1,0:T(8,128)(2,1)}, bf16...) custom-call(bf16[128,2048]{1,0:T(8,128)(2,1)} %tok_hbm.1, ...), custom_call_target="tpu_custom_call" | custom-call | tf_op jit(solution)/shard_map/moe/pallas_call | solution.py:332
  99.9 6.9 %weight_grads.1 = (bf16[128,2048]{1,0:T(8,128)(2,1)}, bf16[128,2048]{1,0:T(8,128)(2,1)}, f32[3072,128]{1,0:T(8,128)}, f32[3072,128]{1,0:T(8,128)}, f32[3072,128]{1,0:T(8,128)}) custom-call(bf16[128,2048]{1,0:T(8,128)(2,1)} %get-tuple-element.17.out_in, bf16[128,2048]{1,0:T(8,128)(2,1)} %get-tuple-element.18.dx_in, bf16[1024,512]{1,0:T(8,128)(2,1)} %bitcast.19, ...), custom_call_target="tpu_custom_call" | custom-call | tf_op jit(solution)/shard_map/weight_grads/pallas_call | solution.py:360

commit v3 on v2

--- a/solution.py
+++ b/solution.py
@@ -17,7 +17,7 @@
 
 
 def tile_of(size):
-    return 256 if size % 256 == 0 else 128
+    return 512 if size % 512 == 0 else 384 if size % 384 == 0 else 128
 
 
 def kernel(
@@ -231,8 +231,8 @@
     near = pl.ds(pl.multiple_of(side * part, part), part)
     far = pl.ds(pl.multiple_of((1 - side) * part, part), part)
     forward(0, near)
+    forward(1, far)
     backward(0, near)
-    forward(1, far)
     backward(1, far)
 
     finish(o_copies[0] + o_copies[1])

time: 109 us -> 108 us (level)
    pallas_call x1, Pallas kernels: 99.3 us -> 98.1 us  [per_device(): pl.pallas_call(functools.partial(kernel, owners, groups, cap), out_shape=...]
where the time goes in v3:
time: 108 us; the launch traced here: 106 us
  Pallas kernels  105 us (97%)
    pallas_call x1, Pallas kernels, per_device(): pl.pallas_call(functools.partial(kernel, owners, groups, cap), out_shape=...  98.1 us
    pallas_call x1, Pallas kernels, per_device(): pl.pallas_call(weight_grads, out_shape=[jax.ShapeDtypeStruct((toks, width...  7.18 us

profile of v3, /device:TPU:13, one launch (start us, length us, event | category | flops | bytes accessed | tf_op | source)
XLA Modules:
  0.0 105.9 jit_solution(14305035787132067020)
XLA Ops:
  0.6 98.1 %moe.1 = (bf16[128,2048]{1,0:T(8,128)(2,1)}, bf16[128,2048]{1,0:T(8,128)(2,1)}, bf16[4,256,512]{2,1,0:T(8,128)(2,1)}, bf16[4,256,512]{2,1,0:T(8,128)(2,1)}, bf16...) custom-call(bf16[128,2048]{1,0:T(8,128)(2,1)} %tok_hbm.1, ...), custom_call_target="tpu_custom_call" | custom-call | tf_op jit(solution)/shard_map/moe/pallas_call | solution.py:332
  98.7 7.2 %weight_grads.1 = (bf16[128,2048]{1,0:T(8,128)(2,1)}, bf16[128,2048]{1,0:T(8,128)(2,1)}, f32[3072,128]{1,0:T(8,128)}, f32[3072,128]{1,0:T(8,128)}, f32[3072,128]{1,0:T(8,128)}) custom-call(bf16[128,2048]{1,0:T(8,128)(2,1)} %get-tuple-element.17.out_in, bf16[128,2048]{1,0:T(8,128)(2,1)} %get-tuple-element.18.dx_in, bf16[1024,512]{1,0:T(8,128)(2,1)} %bitcast.19, ...), custom_call_target="tpu_custom_call" | custom-call | tf_op jit(solution)/shard_map/weight_grads/pallas_call | solution.py:360
